TPU v7x, 512 devices: a whole 4x4x16 slice. The times are simulated.
512 devices in a mesh: brow: 16 (over z), bcol: 32 (over y, x, core).
Axes of the slice: x: 4, y: 4, z: 16, core: 2. Of those that a mesh axis runs over, the one named last changes fastest.
Arguments:
- ancestor_cov: bfloat16 [5632, 5632], P('brow', 'bcol'), may hold values from -1 to 4
- ancestor_pattern: int32 [22], replicated, may hold values 0 or 1
- parent_panel: bfloat16 [5632, 4096], P('brow'), may hold values from -0.5 to 0.5
- parent_inverse: bfloat16 [4096, 4096], P('brow', 'bcol'), may hold values from -1 to 4
- child_pattern: int32 [16], replicated, may hold values 0 or 1
- child_panel: bfloat16 [4096, 4096], P('brow', 'bcol'), may hold values from -0.3125 to 0.3125
- child_inverse: bfloat16 [4096, 4096], P('brow', 'bcol'), may hold values from -1 to 4
Outputs:
- ancestor_block: bfloat16 [5632, 4096], P('brow', 'bcol')
- parent_diag: bfloat16 [4096, 4096], P('brow', 'bcol')
- parent_child: bfloat16 [4096, 4096], P('brow', 'bcol')
- child_diag: bfloat16 [4096, 4096], P('brow', 'bcol')
All inputs are finite; a program needn't handle non-finite values.
Results may differ from a plain program's by a relative error of at most 0.006.
Values may be sent and summed in bfloat16 or wider, within the bound.
No kernel may reach another device: no remote copies, remote signals or barrier semaphores. Data moves between devices by JAX's collectives and lax.ppermute only.
A program may use at most 64 MiB of HBM per device.

v0:
```python
import jax
import jax.numpy as jnp
from jax import lax
from jax.sharding import PartitionSpec as P


def block_keep(pattern, first_row, count, total_rows):
    block_rows = total_rows // pattern.shape[0]
    row_ids = first_row + lax.iota(jnp.int32, count)
    block_ids = lax.iota(jnp.int32, pattern.shape[0])
    matches = row_ids[:, None] // block_rows == block_ids[None, :]
    return jnp.sum(jnp.where(matches, pattern[None, :], 0), axis=1)


def per_device(
    ancestor_cov,
    ancestor_pattern,
    parent_panel,
    parent_inverse,
    child_pattern,
    child_panel,
    child_inverse,
):
    row_index = lax.axis_index("brow")
    column_index = lax.axis_index("bcol")
    row_devices = lax.axis_size("brow")
    local_rows = parent_panel.shape[0]
    band_rows = parent_inverse.shape[0]
    band_columns = parent_inverse.shape[1]
    ancestor_keep = block_keep(
        ancestor_pattern, row_index * local_rows, local_rows, local_rows * row_devices
    )
    child_keep = block_keep(
        child_pattern, row_index * band_rows, band_rows, band_rows * row_devices
    )
    parent_masked = parent_panel * ancestor_keep[:, None].astype(jnp.bfloat16)
    child_masked = child_panel * child_keep[:, None].astype(jnp.bfloat16)
    panel_slab = lax.dynamic_slice_in_dim(
        parent_masked, column_index * band_columns, band_columns, 1
    )
    parent_columns, child_columns = (
        lax.all_gather(panel_slab, "brow", axis=0, tiled=True),
        lax.all_gather(child_masked, "brow", axis=0, tiled=True),
    )
    factor_rows = parent_columns
    ancestor_sum = jnp.dot(
        lax.all_gather(ancestor_cov, "bcol", axis=1, tiled=True),
        factor_rows,
        preferred_element_type=jnp.float32,
    )
    ancestor_block = (-ancestor_sum * ancestor_keep[:, None].astype(jnp.float32)).astype(
        jnp.bfloat16
    )
    parent_wide = lax.all_to_all(parent_masked, "brow", split_axis=1, concat_axis=0, tiled=True)
    image_band = lax.all_gather(ancestor_block, "brow", axis=0, tiled=True)
    parent_inner = jnp.einsum(
        "ka,kb->ab", parent_wide, image_band, preferred_element_type=jnp.float32
    )
    parent_diag = (parent_inverse.astype(jnp.float32) - parent_inner).astype(jnp.bfloat16)
    factor_rows = child_columns
    parent_sum = jnp.dot(
        lax.all_gather(parent_diag, "bcol", axis=1, tiled=True),
        factor_rows,
        preferred_element_type=jnp.float32,
    )
    parent_child = (-parent_sum * child_keep[:, None].astype(jnp.float32)).astype(jnp.bfloat16)
    child_band = lax.all_gather(child_masked, "bcol", axis=1, tiled=True)
    child_inner = lax.psum_scatter(
        jnp.einsum("ka,kb->ab", child_band, parent_child, preferred_element_type=jnp.float32),
        "brow",
        scatter_dimension=0,
        tiled=True,
    )
    child_diag = (child_inverse.astype(jnp.float32) - child_inner).astype(jnp.bfloat16)
    return (ancestor_block, parent_diag, parent_child, child_diag)


def solution(mesh):
    return jax.shard_map(
        per_device,
        mesh=mesh,
        in_specs=(
            P("brow", "bcol"),
            P(),
            P("brow", None),
            P("brow", "bcol"),
            P(),
            P("brow", "bcol"),
            P("brow", "bcol"),
        ),
        out_specs=(P("brow", "bcol"), P("brow", "bcol"), P("brow", "bcol"), P("brow", "bcol")),
        check_vma=False,
    )
```

profile of v0, /device:TPU:8, one launch (start us, length us, event | category | flops | bytes accessed | tf_op | source)
XLA Modules:
  0.0 577.8 jit_solution(14311863399539205714)
XLA Ops:
  7.2 0.7 select_reduce_fusion
  8.0 2.1 broadcast_multiply_fusion
  10.1 0.7 constant_dynamic-slice_fusion
  10.8 0.7 all-gather.9.cloned.1.call-update
  11.5 1.9 copy.16
  13.4 15.2 %all-to-all-start = ((bf16[352,16,256]{2,0,1:T(8,128)(2,1)}), bf16[352,16,256]{2,0,1:T(8,128)(2,1)S(1)}, u32[]{:S(2)}, u32[]{:S(2)}) async-start(bf16[352,16,256]{2,0,1:T(8,128)(2,1)} %bitcast.19), calls=%async_computation | async-start | bytes 5767168 | tf_op jit(solution)/shard_map/all_to_all | solution.py:54
  28.6 0.0 all-gather.11.cloned.1.call-start
  28.7 119.7 %all-gather.7.cloned.1.call-done = bf16[5632,128]{1,0:T(8,128)(2,1)} async-done(((bf16[352,128]{1,0:T(8,128)(2,1)}), bf16[5632,128]{1,0:T(8,128)(2,1)}) %all-gather.7.cloned.1.call-update) | async-done | bytes 1441808 | tf_op jit(solution)/shard_map/all_gather | solution.py:42
  148.3 73.0 %all-gather.9.cloned.1.call-done = bf16[352,5632]{0,1:T(8,128)(2,1)} async-done(((bf16[352,176]{0,1:T(8,128)(2,1)}), bf16[352,5632]{0,1:T(8,128)(2,1)}) %all-gather.9.cloned.1.call-update) | async-done | bytes 3964944 | tf_op jit(solution)/shard_map/all_gather | solution.py:47
  221.3 5.1 fusion.5
  226.4 0.0 all-gather.15.cloned.1.call-start
  226.5 0.1 select_reduce_fusion.1
  226.6 0.7 broadcast_multiply_fusion.1
  227.4 0.0 all-gather.13.cloned.1.call-start
  227.4 71.0 %all-gather.11.cloned.1.call-done = bf16[5632,128]{1,0:T(8,128)(2,1)} async-done(((bf16[352,128]{1,0:T(8,128)(2,1)}), bf16[5632,128]{1,0:T(8,128)(2,1)}) %all-gather.11.cloned.1.call-update) | async-done | bytes 1441808 | tf_op jit(solution)/shard_map/all_gather | solution.py:55
  298.4 2.9 fusion.3
  301.4 0.5 all-gather.17.cloned.1.call-update
  302.0 66.9 %all-gather.15.cloned.1.call-done = bf16[4096,128]{1,0:T(8,128)(2,1)} async-done(((bf16[256,128]{1,0:T(8,128)(2,1)}), bf16[4096,128]{1,0:T(8,128)(2,1)}) %all-gather.15.cloned.1.call-update) | async-done | bytes 1048592 | tf_op jit(solution)/shard_map/all_gather | solution.py:43
  368.9 60.1 %all-gather.13.cloned.1.call-done = bf16[256,4096]{1,0:T(8,128)(2,1)} async-done(((bf16[256,128]{1,0:T(8,128)(2,1)}), bf16[256,4096]{1,0:T(8,128)(2,1)}) %all-gather.13.cloned.1.call-update) | async-done | bytes 2097168 | tf_op jit(solution)/shard_map/all_gather | solution.py:62
  429.0 2.6 fusion.4
  431.6 60.5 %all-gather.17.cloned.1.call-done = bf16[256,4096]{1,0:T(8,128)(2,1)} async-done(((bf16[256,128]{1,0:T(8,128)(2,1)}), bf16[256,4096]{1,0:T(8,128)(2,1)}) %all-gather.17.cloned.1.call-update) | async-done | bytes 2097168 | tf_op jit(solution)/shard_map/all_gather | solution.py:67
  492.2 3.7 fusion.11
  495.8 73.5 %reduce-scatter.2.cloned.1.call-done = f32[256,128]{1,0:T(8,128)} async-done(((f32[4096,128]{1,0:T(8,128)}), f32[256,128]{1,0:T(8,128)}) %reduce-scatter.2.cloned.1.call-update) | async-done | bytes 131088 | tf_op jit(solution)/shard_map/reduce_scatter | solution.py:68
  569.4 1.5 subtract_convert_fusion
  (24 shorter events, 0.3 us)
Async XLA Ops:
  7.2 141.2 %all-gather.7.cloned.1.call-start = ((), (), s32[]{:S(2)}) async-start(), calls=%async_computation.2 | async-start | bytes 1531904 | tf_op jit(solution)/shard_map/all_gather | solution.py:42
  10.8 210.5 %all-gather.9.cloned.1.call-start = ((), (), s32[]{:S(2)}) async-start(), calls=%async_computation.3 | async-start | bytes 4460544 | tf_op jit(solution)/shard_map/all_gather | solution.py:47
  13.4 285.0 %all-to-all-start = ((bf16[352,16,256]{2,0,1:T(8,128)(2,1)}), bf16[352,16,256]{2,0,1:T(8,128)(2,1)S(1)}, u32[]{:S(2)}, u32[]{:S(2)}) async-start(bf16[352,16,256]{2,0,1:T(8,128)(2,1)} %bitcast.19), calls=%async_computation | async-start | bytes 5767168 | tf_op jit(solution)/shard_map/all_to_all | solution.py:54
  28.6 269.8 %all-gather.11.cloned.1.call-start = ((), (), s32[]{:S(2)}) async-start(), calls=%async_computation.4 | async-start | bytes 1531904 | tf_op jit(solution)/shard_map/all_gather | solution.py:55
  221.3 5.2 copy-start.4
  221.3 5.3 copy-start.2
  221.3 77.1 %copy-start.1 = (bf16[256,128]{1,0:T(8,128)(2,1)S(1)}, bf16[256,128]{1,0:T(8,128)(2,1)}, u32[]{:S(2)}) copy-start(bf16[256,128]{1,0:T(8,128)(2,1)} %param.10) | copy-start | bytes 196612
  226.4 142.5 %all-gather.15.cloned.1.call-start = ((), (), s32[]{:S(2)}) async-start(), calls=%async_computation.6 | async-start | bytes 1114112 | tf_op jit(solution)/shard_map/all_gather | solution.py:43
  227.4 201.7 %all-gather.13.cloned.1.call-start = ((), (), s32[]{:S(2)}) async-start(), calls=%async_computation.5 | async-start | bytes 2162688 | tf_op jit(solution)/shard_map/all_gather | solution.py:62
  301.4 190.8 %all-gather.17.cloned.1.call-start = ((), (), s32[]{:S(2)}) async-start(), calls=%async_computation.7 | async-start | bytes 2162688 | tf_op jit(solution)/shard_map/all_gather | solution.py:67
  302.0 267.4 %reduce-scatter.2.cloned.1.call-start = ((), (), s32[]{:S(2)}) async-start(), calls=%async_computation.8 | async-start | bytes 2228224 | tf_op jit(solution)/shard_map/reduce_scatter | solution.py:68
  431.6 64.2 %copy-start = (bf16[256,128]{1,0:T(8,128)(2,1)}, bf16[256,128]{1,0:T(8,128)(2,1)S(1)}, u32[]{:S(2)}) copy-start(bf16[256,128]{1,0:T(8,128)(2,1)S(1)} %fusion.4) | copy-start | bytes 196612
  495.8 73.6 %copy-start.3 = (bf16[256,128]{1,0:T(8,128)(2,1)S(1)}, bf16[256,128]{1,0:T(8,128)(2,1)}, u32[]{:S(2)}) copy-start(bf16[256,128]{1,0:T(8,128)(2,1)} %param.13) | copy-start | bytes 196612
Sparse Core Ops, SparseCore 0:
  10.9 137.3 all-gather.6
  151.5 69.7 all-gather.8
  226.5 71.8 all-gather.10
  300.9 67.9 all-gather.14
  372.4 56.5 all-gather.12
  432.5 59.5 all-gather.16
  496.0 73.3 reduce-scatter.1
where the time goes:
time: 578 us
  waiting for transfers between devices  526 us (91%)
  starting transfers between devices  15.5 us (3%)
  matrix products  14.2 us (2%)
  between operations  14.2 us (2%)
    all_gather x1, waiting for transfers between devices, per_device(): lax.all_gather(panel_slab, 'brow', axis=0, tiled=True)  120 us
    reduce_scatter x1, waiting for transfers between devices, per_device(): lax.psum_scatter(jnp.einsum('ka,kb->ab', child_band, parent_child, prefer...  73.5 us
    all_gather x1, waiting for transfers between devices, per_device(): lax.all_gather(ancestor_cov, 'bcol', axis=1, tiled=True)  73 us
    all_gather x1, waiting for transfers between devices, per_device(): image_band = lax.all_gather(ancestor_block, 'brow', axis=0, tiled=True)  71 us
    all_gather x1, waiting for transfers between devices, per_device(): lax.all_gather(child_masked, 'brow', axis=0, tiled=True)  66.9 us
    all_gather x1, waiting for transfers between devices, per_device(): child_band = lax.all_gather(child_masked, 'bcol', axis=1, tiled=True)  60.5 us
    all_gather x1, waiting for transfers between devices, per_device(): lax.all_gather(parent_diag, 'bcol', axis=1, tiled=True)  60.1 us
    all_to_all x1, starting transfers between devices, per_device(): lax.all_to_all(parent_masked, 'brow', split_axis=1, concat_axis=0, tiled=...  15.2 us
  transfers between devices with their start and end apart: 8, of which 7 were waited for; matrix products, arithmetic and copies ran while one was open for 2% of the time, Pallas kernels for 0%

commit v1 on v0

--- a/solution.py
+++ b/solution.py
@@ -2,6 +2,19 @@
 import jax.numpy as jnp
 from jax import lax
 from jax.sharding import PartitionSpec as P
+
+
+def collect(x, axis, dim):
+    ways = lax.axis_size(axis)
+    up = [(d, (d + 1) % ways) for d in range(ways)]
+    down = [(d, (d - 1) % ways) for d in range(ways)]
+    earlier, later = ([x], [x])
+    for _ in range(ways // 2):
+        earlier.append(lax.ppermute(earlier[-1], axis, up))
+    for _ in range((ways - 1) // 2):
+        later.append(lax.ppermute(later[-1], axis, down))
+    line = jnp.concatenate([*earlier[::-1], *later[1:]], axis=dim)
+    return jnp.roll(line, (lax.axis_index(axis) - ways // 2) * x.shape[dim], axis=dim)
 
 
 def block_keep(pattern, first_row, count, total_rows):
@@ -39,7 +52,7 @@
         parent_masked, column_index * band_columns, band_columns, 1
     )
     parent_columns, child_columns = (
-        lax.all_gather(panel_slab, "brow", axis=0, tiled=True),
+        collect(panel_slab, "brow", 0),
         lax.all_gather(child_masked, "brow", axis=0, tiled=True),
     )
     factor_rows = parent_columns

time: 578 us -> 598 us (1.035)
  waiting for transfers between devices: 526 us -> 461 us
  starting transfers between devices: 15.5 us -> 68.8 us
  local copies, waits for them, and re-layouts: 2.59 us -> 32.3 us
    ppermute x0 -> x15, waiting for transfers between devices: none -> 130 us  [the longest x8 130 us: collect(): earlier.append(lax.ppermute(earlier[-1], axis, up))]
    all_gather x1 -> x0, waiting for transfers between devices: 120 us -> none  [per_device(): lax.all_gather(panel_slab, 'brow', axis=0, tiled=True)]
    all_gather x1, waiting for transfers between devices: 73 us -> 0.01 us  [per_device(): lax.all_gather(ancestor_cov, 'bcol', axis=1, tiled=True)]
    ppermute x0 -> x15, starting transfers between devices: none -> 53.4 us  [the longest x7 36.2 us: collect(): later.append(lax.ppermute(later[-1], axis, down))]
    unnamed x10 -> x53, local copies, waits for them, and re-layouts: 0.02 us -> 29.7 us
  transfers between devices with their start and end apart: 8 -> 22, of which waited for: 7 -> 13; matrix products, arithmetic and copies ran while one was open for 2% -> 8% of each run, Pallas kernels for 0% -> 0%
where the time goes in v1:
time: 598 us; the launch traced here: 597 us
  waiting for transfers between devices  461 us (77%)
  starting transfers between devices  68.8 us (12%)
  local copies, waits for them, and re-layouts  32.3 us (5%)
  matrix products  15.2 us (3%)
  between operations  14.5 us (2%)
    ppermute x8, waiting for transfers between devices, collect(): earlier.append(lax.ppermute(earlier[-1], axis, up))  130 us
    reduce_scatter x1, waiting for transfers between devices, per_device(): lax.psum_scatter(jnp.einsum('ka,kb->ab', child_band, parent_child, prefer...  73.5 us
    all_gather x1, waiting for transfers between devices, per_device(): image_band = lax.all_gather(ancestor_block, 'brow', axis=0, tiled=True)  68.9 us
    all_gather x1, waiting for transfers between devices, per_device(): lax.all_gather(child_masked, 'brow', axis=0, tiled=True)  66.2 us
    all_gather x1, waiting for transfers between devices, per_device(): child_band = lax.all_gather(child_masked, 'bcol', axis=1, tiled=True)  60.5 us
    all_gather x1, waiting for transfers between devices, per_device(): lax.all_gather(parent_diag, 'bcol', axis=1, tiled=True)  60.1 us
    ppermute x7, starting transfers between devices, collect(): later.append(lax.ppermute(later[-1], axis, down))  36.2 us
    unnamed x53, local copies, waits for them, and re-layouts  29.7 us
  transfers between devices with their start and end apart: 22, of which 13 were waited for; matrix products, arithmetic and copies ran while one was open for 8% of the time, Pallas kernels for 0%

profile of v1, /device:TPU:8, one launch (start us, length us, event | category | flops | bytes accessed | tf_op | source)
XLA Modules:
  0.0 596.9 jit_solution(15054384902468916493)
XLA Ops:
  8.7 2.1 broadcast_multiply_fusion
  10.8 1.9 copy.16
  12.7 15.2 %all-to-all-start = ((bf16[352,16,256]{2,0,1:T(8,128)(2,1)}), bf16[352,16,256]{2,0,1:T(8,128)(2,1)}, u32[]{:S(2)}, u32[]{:S(2)}) async-start(bf16[352,16,256]{2,0,1:T(8,128)(2,1)} %bitcast.17), calls=%async_computation | async-start | bytes 5767168 | tf_op jit(solution)/shard_map/all_to_all | solution.py:67
  28.0 3.8 collective-permute-start
  31.8 125.2 %collective-permute-done = bf16[352,128]{1,0:T(8,128)(2,1)S(1)} collective-permute-done((bf16[352,128]{1,0:T(8,128)(2,1)S(1)}, bf16[352,128]{1,0:T(8,128)(2,1)S(1)}, u32[]{:S(2)}, u32[]{:S(2)}) %collective-permute-start) | collective-permute-done | bytes 90144 | tf_op jit(solution)/shard_map/ppermute | solution.py:13
  158.9 5.1 collective-permute-start.8
  166.6 5.1 collective-permute-start.9
  174.2 5.1 collective-permute-start.10
  181.8 5.1 collective-permute-start.11
  187.5 1.9 collective-permute-start.5
  189.4 5.1 collective-permute-start.12
  195.9 1.9 collective-permute-start.6
  197.8 5.3 collective-permute-start.13
  204.0 1.9 collective-permute-start.7
  205.9 5.3 collective-permute-start.14
  242.3 5.1 fusion.14
  248.4 68.9 %all-gather.8.cloned.1.call-done = bf16[5632,128]{1,0:T(8,128)(2,1)} async-done(((bf16[352,128]{1,0:T(8,128)(2,1)}), bf16[5632,128]{1,0:T(8,128)(2,1)}) %all-gather.8.cloned.1.call-update) | async-done | bytes 1441808 | tf_op jit(solution)/shard_map/all_gather | solution.py:68
  317.3 3.8 fusion.12
  321.8 66.2 %all-gather.12.cloned.1.call-done = bf16[4096,128]{1,0:T(8,128)(2,1)} async-done(((bf16[256,128]{1,0:T(8,128)(2,1)}), bf16[4096,128]{1,0:T(8,128)(2,1)}) %all-gather.12.cloned.1.call-update) | async-done | bytes 1048592 | tf_op jit(solution)/shard_map/all_gather | solution.py:56
  388.0 60.1 %all-gather.10.cloned.1.call-done = bf16[256,4096]{1,0:T(8,128)(2,1)} async-done(((bf16[256,128]{1,0:T(8,128)(2,1)}), bf16[256,4096]{1,0:T(8,128)(2,1)}) %all-gather.10.cloned.1.call-update) | async-done | bytes 2097168 | tf_op jit(solution)/shard_map/all_gather | solution.py:75
  448.1 2.6 fusion.13
  450.7 60.5 %all-gather.14.cloned.1.call-done = bf16[256,4096]{1,0:T(8,128)(2,1)} async-done(((bf16[256,128]{1,0:T(8,128)(2,1)}), bf16[256,4096]{1,0:T(8,128)(2,1)}) %all-gather.14.cloned.1.call-update) | async-done | bytes 2097168 | tf_op jit(solution)/shard_map/all_gather | solution.py:80
  511.2 3.7 fusion.23
  514.9 73.5 %reduce-scatter.2.cloned.1.call-done = f32[256,128]{1,0:T(8,128)} async-done(((f32[4096,128]{1,0:T(8,128)}), f32[256,128]{1,0:T(8,128)}) %reduce-scatter.2.cloned.1.call-update) | async-done | bytes 131088 | tf_op jit(solution)/shard_map/reduce_scatter | solution.py:81
  (95 shorter events, 47.8 us)
Async XLA Ops:
  7.2 235.1 %all-gather.6.cloned.1.call-start = ((), (), s32[]{:S(2)}) async-start(), calls=%async_computation.2 | async-start | bytes 4460544 | tf_op jit(solution)/shard_map/all_gather | solution.py:60
  12.7 304.6 %all-to-all-start = ((bf16[352,16,256]{2,0,1:T(8,128)(2,1)}), bf16[352,16,256]{2,0,1:T(8,128)(2,1)}, u32[]{:S(2)}, u32[]{:S(2)}) async-start(bf16[352,16,256]{2,0,1:T(8,128)(2,1)} %bitcast.17), calls=%async_computation | async-start | bytes 5767168 | tf_op jit(solution)/shard_map/all_to_all | solution.py:67
  27.9 289.4 %all-gather.8.cloned.1.call-start = ((), (), s32[]{:S(2)}) async-start(), calls=%async_computation.3 | async-start | bytes 1531904 | tf_op jit(solution)/shard_map/all_gather | solution.py:68
  28.0 129.0 %collective-permute-start = (bf16[352,128]{1,0:T(8,128)(2,1)S(1)}, bf16[352,128]{1,0:T(8,128)(2,1)S(1)}, u32[]{:S(2)}, u32[]{:S(2)}) collective-permute-start(bf16[352,128]{1,0:T(8,128)(2,1)S(1)} %constant_dynamic-slice_fusion), channel_id=1, source_target_pairs={{0,32},{32,64},{64,96},{96,128},{128,160},{160,192},{192,224},{224... | collective-permute-start | bytes 270344 | tf_op jit(solution)/shard_map/ppermute | solution.py:13
  157.0 7.6 %collective-permute-start.1 = (bf16[352,128]{1,0:T(8,128)(2,1)S(1)}, bf16[352,128]{1,0:T(8,128)(2,1)S(1)}, u32[]{:S(2)}, u32[]{:S(2)}) collective-permute-start(bf16[352,128]{1,0:T(8,128)(2,1)S(1)} %collective-permute-done), channel_id=1, source_target_pairs={{0,32},{32,64},{64,96},{96,128},{128,160},{160,192},{192,224},{224... | collective-permute-start | bytes 270344 | tf_op jit(solution)/shard_map/ppermute | solution.py:13
  158.9 7.6 %collective-permute-start.8 = (bf16[352,128]{1,0:T(8,128)(2,1)S(1)}, bf16[352,128]{1,0:T(8,128)(2,1)S(1)}, u32[]{:S(2)}, u32[]{:S(2)}) collective-permute-start(bf16[352,128]{1,0:T(8,128)(2,1)S(1)} %constant_dynamic-slice_fusion), channel_id=1, source_target_pairs={{0,480},{32,0},{64,32},{96,64},{128,96},{160,128},{192,160},{224,1... | collective-permute-start | bytes 270344 | tf_op jit(solution)/shard_map/ppermute | solution.py:15
  164.6 7.6 %collective-permute-start.2 = (bf16[352,128]{1,0:T(8,128)(2,1)S(1)}, bf16[352,128]{1,0:T(8,128)(2,1)S(1)}, u32[]{:S(2)}, u32[]{:S(2)}) collective-permute-start(bf16[352,128]{1,0:T(8,128)(2,1)S(1)} %collective-permute-done.1), channel_id=1, source_target_pairs={{0,32},{32,64},{64,96},{96,128},{128,160},{160,192},{192,224},{224... | collective-permute-start | bytes 270344 | tf_op jit(solution)/shard_map/ppermute | solution.py:13
  166.6 7.6 %collective-permute-start.9 = (bf16[352,128]{1,0:T(8,128)(2,1)S(1)}, bf16[352,128]{1,0:T(8,128)(2,1)S(1)}, u32[]{:S(2)}, u32[]{:S(2)}) collective-permute-start(bf16[352,128]{1,0:T(8,128)(2,1)S(1)} %collective-permute-done.8), channel_id=1, source_target_pairs={{0,480},{32,0},{64,32},{96,64},{128,96},{160,128},{192,160},{224,1... | collective-permute-start | bytes 270344 | tf_op jit(solution)/shard_map/ppermute | solution.py:15
  172.3 7.6 %collective-permute-start.3 = (bf16[352,128]{1,0:T(8,128)(2,1)S(1)}, bf16[352,128]{1,0:T(8,128)(2,1)S(1)}, u32[]{:S(2)}, u32[]{:S(2)}) collective-permute-start(bf16[352,128]{1,0:T(8,128)(2,1)S(1)} %collective-permute-done.2), channel_id=1, source_target_pairs={{0,32},{32,64},{64,96},{96,128},{128,160},{160,192},{192,224},{224... | collective-permute-start | bytes 270344 | tf_op jit(solution)/shard_map/ppermute | solution.py:13
  174.2 7.6 %collective-permute-start.10 = (bf16[352,128]{1,0:T(8,128)(2,1)S(1)}, bf16[352,128]{1,0:T(8,128)(2,1)S(1)}, u32[]{:S(2)}, u32[]{:S(2)}) collective-permute-start(bf16[352,128]{1,0:T(8,128)(2,1)S(1)} %collective-permute-done.9), channel_id=1, source_target_pairs={{0,480},{32,0},{64,32},{96,64},{128,96},{160,128},{192,160},{224,1... | collective-permute-start | bytes 270344 | tf_op jit(solution)/shard_map/ppermute | solution.py:15
  179.9 7.6 %collective-permute-start.4 = (bf16[352,128]{1,0:T(8,128)(2,1)S(1)}, bf16[352,128]{1,0:T(8,128)(2,1)S(1)}, u32[]{:S(2)}, u32[]{:S(2)}) collective-permute-start(bf16[352,128]{1,0:T(8,128)(2,1)S(1)} %collective-permute-done.3), channel_id=1, source_target_pairs={{0,32},{32,64},{64,96},{96,128},{128,160},{160,192},{192,224},{224... | collective-permute-start | bytes 270344 | tf_op jit(solution)/shard_map/ppermute | solution.py:13
  181.8 7.6 %collective-permute-start.11 = (bf16[352,128]{1,0:T(8,128)(2,1)S(1)}, bf16[352,128]{1,0:T(8,128)(2,1)S(1)}, u32[]{:S(2)}, u32[]{:S(2)}) collective-permute-start(bf16[352,128]{1,0:T(8,128)(2,1)S(1)} %collective-permute-done.10), channel_id=1, source_target_pairs={{0,480},{32,0},{64,32},{96,64},{128,96},{160,128},{192,160},{224,1... | collective-permute-start | bytes 270344 | tf_op jit(solution)/shard_map/ppermute | solution.py:15
  187.5 8.4 %collective-permute-start.5 = (bf16[352,128]{1,0:T(8,128)(2,1)S(1)}, bf16[352,128]{1,0:T(8,128)(2,1)S(1)}, u32[]{:S(2)}, u32[]{:S(2)}) collective-permute-start(bf16[352,128]{1,0:T(8,128)(2,1)S(1)} %collective-permute-done.4), channel_id=1, source_target_pairs={{0,32},{32,64},{64,96},{96,128},{128,160},{160,192},{192,224},{224... | collective-permute-start | bytes 270344 | tf_op jit(solution)/shard_map/ppermute | solution.py:13
  189.4 8.4 %collective-permute-start.12 = (bf16[352,128]{1,0:T(8,128)(2,1)S(1)}, bf16[352,128]{1,0:T(8,128)(2,1)}, u32[]{:S(2)}, u32[]{:S(2)}) collective-permute-start(bf16[352,128]{1,0:T(8,128)(2,1)S(1)} %collective-permute-done.11), channel_id=1, source_target_pairs={{0,480},{32,0},{64,32},{96,64},{128,96},{160,128},{192,160},{224,1... | collective-permute-start | bytes 270344 | tf_op jit(solution)/shard_map/ppermute | solution.py:15
  195.9 8.1 %collective-permute-start.6 = (bf16[352,128]{1,0:T(8,128)(2,1)S(1)}, bf16[352,128]{1,0:T(8,128)(2,1)}, u32[]{:S(2)}, u32[]{:S(2)}) collective-permute-start(bf16[352,128]{1,0:T(8,128)(2,1)S(1)} %collective-permute-done.5), channel_id=1, source_target_pairs={{0,32},{32,64},{64,96},{96,128},{128,160},{160,192},{192,224},{224... | collective-permute-start | bytes 270344 | tf_op jit(solution)/shard_map/ppermute | solution.py:13
  197.8 8.1 %collective-permute-start.13 = (bf16[352,128]{1,0:T(8,128)(2,1)}, bf16[352,128]{1,0:T(8,128)(2,1)}, u32[]{:S(2)}, u32[]{:S(2)}) collective-permute-start(bf16[352,128]{1,0:T(8,128)(2,1)} %collective-permute-done.12), channel_id=1, source_target_pairs={{0,480},{32,0},{64,32},{96,64},{128,96},{160,128},{192,160},{224,1... | collective-permute-start | bytes 270344 | tf_op jit(solution)/shard_map/ppermute | solution.py:15
  204.0 7.9 %collective-permute-start.7 = (bf16[352,128]{1,0:T(8,128)(2,1)}, bf16[352,128]{1,0:T(8,128)(2,1)}, u32[]{:S(2)}, u32[]{:S(2)}) collective-permute-start(bf16[352,128]{1,0:T(8,128)(2,1)} %collective-permute-done.6), channel_id=1, source_target_pairs={{0,32},{32,64},{64,96},{96,128},{128,160},{160,192},{192,224},{224... | collective-permute-start | bytes 270344 | tf_op jit(solution)/shard_map/ppermute | solution.py:13
  205.9 21.8 %collective-permute-start.14 = (bf16[352,128]{1,0:T(8,128)(2,1)}, bf16[352,128]{1,0:T(8,128)(2,1)S(1)}, u32[]{:S(2)}, u32[]{:S(2)}) collective-permute-start(bf16[352,128]{1,0:T(8,128)(2,1)} %collective-permute-done.13), channel_id=1, source_target_pairs={{0,480},{32,0},{64,32},{96,64},{128,96},{160,128},{192,160},{224,1... | collective-permute-start | bytes 270344 | tf_op jit(solution)/shard_map/ppermute | solution.py:15
  242.2 75.1 %copy-start.7 = (bf16[256,128]{1,0:T(8,128)(2,1)S(1)}, bf16[256,128]{1,0:T(8,128)(2,1)}, u32[]{:S(2)}) copy-start(bf16[256,128]{1,0:T(8,128)(2,1)} %param.10) | copy-start | bytes 196612
  247.4 140.6 %all-gather.12.cloned.1.call-start = ((), (), s32[]{:S(2)}) async-start(), calls=%async_computation.5 | async-start | bytes 1114112 | tf_op jit(solution)/shard_map/all_gather | solution.py:56
  248.3 199.8 %all-gather.10.cloned.1.call-start = ((), (), s32[]{:S(2)}) async-start(), calls=%async_computation.4 | async-start | bytes 2162688 | tf_op jit(solution)/shard_map/all_gather | solution.py:75
  321.2 190.1 %all-gather.14.cloned.1.call-start = ((), (), s32[]{:S(2)}) async-start(), calls=%async_computation.6 | async-start | bytes 2162688 | tf_op jit(solution)/shard_map/all_gather | solution.py:80
  321.8 266.7 %reduce-scatter.2.cloned.1.call-start = ((), (), s32[]{:S(2)}) async-start(), calls=%async_computation.7 | async-start | bytes 2228224 | tf_op jit(solution)/shard_map/reduce_scatter | solution.py:81
  450.7 137.8 %copy-start.9 = (bf16[256,128]{1,0:T(8,128)(2,1)S(1)}, bf16[256,128]{1,0:T(8,128)(2,1)}, u32[]{:S(2)}) copy-start(bf16[256,128]{1,0:T(8,128)(2,1)} %param.13) | copy-start | bytes 196612
  (9 other events, 194.9 us)
Sparse Core Ops, SparseCore 0:
  11.2 65.6 all-gather.5
  247.5 69.7 all-gather.7
  320.0 67.9 all-gather.11
  391.5 56.5 all-gather.9
  451.6 59.5 all-gather.13
  515.0 73.3 reduce-scatter.1
